TPU v7x, 32 devices: a whole 2x2x4 slice. The times are simulated.
32 devices in a mesh: dp: 16 (over z, y, x), fsdp: 2 (over core).
Axes of the slice: x: 2, y: 2, z: 4, core: 2. Of those that a mesh axis runs over, the one named last changes fastest.
Arguments:
- tokens: bfloat16 [256, 196, 768], P(('dp', 'fsdp')), may hold values from -6 to 6
- tissue: int32 [256, 196], P(('dp', 'fsdp')), may hold values from 0 to 1, as said below
- norm1_gain: bfloat16 [768], P('fsdp'), may hold values from 0.25 to 1.75
- norm1_shift: bfloat16 [768], P('fsdp'), may hold values from -1.75 to 1.75
- qkv_matrix: bfloat16 [768, 2304], P('fsdp'), may hold values from -0.21875 to 0.21875
- qkv_shift: bfloat16 [1536], P('fsdp'), may hold values from -3 to 3
- proj_matrix: bfloat16 [768, 768], P('fsdp'), may hold values from -0.875 to 0.875
- proj_shift: bfloat16 [768], P('fsdp'), may hold values from -1.75 to 1.75
- norm2_gain: bfloat16 [768], P('fsdp'), may hold values from 0.25 to 1.75
- norm2_shift: bfloat16 [768], P('fsdp'), may hold values from -1.75 to 1.75
- up_matrix: bfloat16 [768, 3072], P('fsdp'), may hold values from -0.21875 to 0.21875
- up_shift: bfloat16 [3072], P('fsdp'), may hold values from -3 to 3
- down_matrix: bfloat16 [3072, 768], P('fsdp'), may hold values from -0.109375 to 0.109375
- down_shift: bfloat16 [768], P('fsdp'), may hold values from -1.75 to 1.75
- cotangent: bfloat16 [256, 196, 768], P(('dp', 'fsdp')), may hold values from -6 to 6
Outputs:
- out_tokens: bfloat16 [256, 196, 768], P(('dp', 'fsdp'))
- tokens_grad: bfloat16 [256, 196, 768], P(('dp', 'fsdp'))
- norm1_gain_grad: float32 [768], P('fsdp')
- norm1_shift_grad: float32 [768], P('fsdp')
- qkv_matrix_grad: float32 [768, 2304], P('fsdp')
- qkv_shift_grad: float32 [1536], P('fsdp')
- proj_matrix_grad: float32 [768, 768], P('fsdp')
- proj_shift_grad: float32 [768], P('fsdp')
- norm2_gain_grad: float32 [768], P('fsdp')
- norm2_shift_grad: float32 [768], P('fsdp')
- up_matrix_grad: float32 [768, 3072], P('fsdp')
- up_shift_grad: float32 [3072], P('fsdp')
- down_matrix_grad: float32 [3072, 768], P('fsdp')
- down_shift_grad: float32 [768], P('fsdp')
Inputs may be any that keep to these rules, and one draw needn't show every extreme that they name: `tissue`: each image has at least one patch slot of value 1.
All inputs are finite; a program needn't handle non-finite values.
Results may differ from a plain program's by a relative error of at most 0.02.
Values may be sent and summed in bfloat16 or wider, within the bound.
A program may use at most 256 MiB of HBM per device.

v0:
```python
import math

import jax
import jax.numpy as jnp
from jax import lax
from jax.sharding import PartitionSpec as P

HEADS = 12
MICRO = 2


norm_eps = 1e-06


def layer_norm(features_in, gain_row, shift_row):
    row_mean = jnp.mean(features_in, axis=-1, keepdims=True)
    centred = features_in - row_mean
    row_var = jnp.mean(centred * centred, axis=-1, keepdims=True)
    return centred * lax.rsqrt(row_var + norm_eps) * gain_row + shift_row


def gelu_exact(hidden):
    return jax.nn.gelu(hidden, approximate=False)


def column_sum(matrix_rows):
    return jnp.sum(matrix_rows.astype(jnp.float32), axis=(0, 1))


def product(rows_in, matrix):
    return jnp.einsum("bpd,de->bpe", rows_in, matrix, preferred_element_type=jnp.float32)


def product_back(rows_in, matrix):
    return jnp.einsum("bpe,de->bpd", rows_in, matrix, preferred_element_type=jnp.float32)


def outer_sum(left_rows, right_rows):
    return jnp.einsum("bpd,bpe->de", left_rows, right_rows, preferred_element_type=jnp.float32)


def attention_scores(queries, key_rows, key_valid, score_scale):
    raw_scores = (
        jnp.einsum("bqhd,bkhd->bhqk", queries, key_rows, preferred_element_type=jnp.float32)
        * score_scale
    )
    return jnp.where(key_valid[:, None, None, :], raw_scores, -1e30)


def run_forward(inputs, tissue_rows, weights):
    (
        norm1_gain,
        norm1_shift,
        qkv_matrix,
        qkv_shift,
        proj_matrix,
        proj_shift,
        norm2_gain,
        norm2_shift,
        up_matrix,
        up_shift,
        down_matrix,
        down_shift,
    ) = weights
    input_float = inputs.astype(jnp.float32)
    images, patches, features = input_float.shape
    head_dim = features // HEADS
    score_scale = 1.0 / math.sqrt(head_dim)
    normed_one, pull_one = jax.vjp(
        layer_norm, input_float, norm1_gain.astype(jnp.float32), norm1_shift.astype(jnp.float32)
    )
    first_in = normed_one.astype(jnp.bfloat16)
    zeros_key = jnp.zeros((features,), jnp.float32)
    shift_all = jnp.concatenate(
        [
            qkv_shift[:features].astype(jnp.float32),
            zeros_key,
            qkv_shift[features:].astype(jnp.float32),
        ]
    )
    qkv_rows = (product(first_in, qkv_matrix) + shift_all).astype(jnp.bfloat16)
    qkv_split = qkv_rows.reshape(images, patches, 3, HEADS, head_dim)
    queries = qkv_split[:, :, 0]
    key_rows = qkv_split[:, :, 1]
    value_rows = qkv_split[:, :, 2]
    key_valid = tissue_rows > 0
    scores = attention_scores(queries, key_rows, key_valid, score_scale)
    row_max = jnp.max(scores, axis=-1, keepdims=True)
    row_total = jnp.sum(jnp.exp(scores - row_max), axis=-1, keepdims=True)
    log_total = row_max + jnp.log(row_total)
    softmax = jnp.exp(scores - log_total)
    mixed_heads = jnp.einsum(
        "bhqk,bkhd->bqhd",
        softmax.astype(jnp.bfloat16),
        value_rows,
        preferred_element_type=jnp.float32,
    )
    weight_rows = tissue_rows.astype(jnp.float32)[:, :, None, None]
    heads_out = (mixed_heads * weight_rows).reshape(images, patches, features).astype(jnp.bfloat16)
    residual = input_float + product(heads_out, proj_matrix) + proj_shift.astype(jnp.float32)
    normed_two, pull_two = jax.vjp(
        layer_norm, residual, norm2_gain.astype(jnp.float32), norm2_shift.astype(jnp.float32)
    )
    second_in = normed_two.astype(jnp.bfloat16)
    hidden = product(second_in, up_matrix) + up_shift.astype(jnp.float32)
    active_float, pull_gelu = jax.vjp(gelu_exact, hidden)
    active = active_float.astype(jnp.bfloat16)
    output_rows = residual + product(active, down_matrix) + down_shift.astype(jnp.float32)
    stored = (
        pull_one,
        first_in,
        queries,
        key_rows,
        value_rows,
        log_total,
        key_valid,
        weight_rows,
        heads_out,
        pull_two,
        second_in,
        pull_gelu,
        active,
    )
    return (output_rows.astype(jnp.bfloat16), stored)


def run_backward(cotangent_rows, stored, weights):
    (
        norm1_gain,
        norm1_shift,
        qkv_matrix,
        qkv_shift,
        proj_matrix,
        proj_shift,
        norm2_gain,
        norm2_shift,
        up_matrix,
        up_shift,
        down_matrix,
        down_shift,
    ) = weights
    (
        pull_one,
        first_in,
        queries,
        key_rows,
        value_rows,
        log_total,
        key_valid,
        weight_rows,
        heads_out,
        pull_two,
        second_in,
        pull_gelu,
        active,
    ) = stored
    images, patches, features = first_in.shape
    head_dim = features // HEADS
    score_scale = 1.0 / math.sqrt(head_dim)
    grad_out = cotangent_rows.astype(jnp.float32)
    grad_down_shift = column_sum(cotangent_rows)
    grad_down = outer_sum(active, cotangent_rows)
    grad_active = product_back(cotangent_rows, down_matrix)
    (grad_hidden,) = pull_gelu(grad_active)
    hidden_low = grad_hidden.astype(jnp.bfloat16)
    grad_up_shift = column_sum(hidden_low)
    grad_up = outer_sum(second_in, hidden_low)
    grad_second = product_back(hidden_low, up_matrix)
    grad_resid_norm, grad_gain_two, grad_shift_two = pull_two(grad_second)
    grad_residual = grad_out + grad_resid_norm
    proj_low = grad_residual.astype(jnp.bfloat16)
    grad_proj_shift = column_sum(proj_low)
    grad_proj = outer_sum(heads_out, proj_low)
    grad_heads = product_back(proj_low, proj_matrix).reshape(images, patches, HEADS, head_dim)
    grad_mixed = (grad_heads * weight_rows).astype(jnp.bfloat16)
    scores = attention_scores(queries, key_rows, key_valid, score_scale)
    softmax = jnp.exp(scores - log_total)
    grad_probs = jnp.einsum(
        "bqhd,bkhd->bhqk", grad_mixed, value_rows, preferred_element_type=jnp.float32
    )
    grad_value = jnp.einsum(
        "bhqk,bqhd->bkhd",
        softmax.astype(jnp.bfloat16),
        grad_mixed,
        preferred_element_type=jnp.float32,
    )
    row_dot = jnp.sum(softmax * grad_probs, axis=-1, keepdims=True)
    grad_scores = (softmax * (grad_probs - row_dot)).astype(jnp.bfloat16)
    grad_query = (
        jnp.einsum("bhqk,bkhd->bqhd", grad_scores, key_rows, preferred_element_type=jnp.float32)
        * score_scale
    )
    grad_key = (
        jnp.einsum("bhqk,bqhd->bkhd", grad_scores, queries, preferred_element_type=jnp.float32)
        * score_scale
    )
    grad_qkv = (
        jnp.stack([grad_query, grad_key, grad_value], axis=2)
        .reshape(images, patches, 3 * features)
        .astype(jnp.bfloat16)
    )
    bias_sums = column_sum(grad_qkv)
    grad_qkv_shift = jnp.concatenate([bias_sums[:features], bias_sums[2 * features :]])
    grad_qkv_matrix = outer_sum(first_in, grad_qkv)
    grad_first = product_back(grad_qkv, qkv_matrix)
    grad_in_norm, grad_gain_one, grad_shift_one = pull_one(grad_first)
    grad_input = (grad_residual + grad_in_norm).astype(jnp.bfloat16)
    gradients = (
        grad_gain_one,
        grad_shift_one,
        grad_qkv_matrix,
        grad_qkv_shift,
        grad_proj,
        grad_proj_shift,
        grad_gain_two,
        grad_shift_two,
        grad_up,
        grad_up_shift,
        grad_down,
        grad_down_shift,
    )
    return (grad_input, gradients)


def add_trees(summed, addend):
    return jax.tree.map(lambda earlier, later: earlier + later, summed, addend)


def on_device(
    tokens,
    tissue,
    norm1_gain,
    norm1_shift,
    qkv_matrix,
    qkv_shift,
    proj_matrix,
    proj_shift,
    norm2_gain,
    norm2_shift,
    up_matrix,
    up_shift,
    down_matrix,
    down_shift,
    cotangent,
):
    per_batch = tokens.shape[0] // MICRO
    owned = None
    output_list = []
    grad_list = []
    for micro_index in range(MICRO):
        lower = micro_index * per_batch
        upper = lower + per_batch
        forward_weights = (
            lax.all_gather(norm1_gain, "fsdp", axis=0, tiled=True),
            lax.all_gather(norm1_shift, "fsdp", axis=0, tiled=True),
            lax.all_gather(qkv_matrix, "fsdp", axis=0, tiled=True),
            lax.all_gather(qkv_shift, "fsdp", axis=0, tiled=True),
            lax.all_gather(proj_matrix, "fsdp", axis=0, tiled=True),
            lax.all_gather(proj_shift, "fsdp", axis=0, tiled=True),
            lax.all_gather(norm2_gain, "fsdp", axis=0, tiled=True),
            lax.all_gather(norm2_shift, "fsdp", axis=0, tiled=True),
            lax.all_gather(up_matrix, "fsdp", axis=0, tiled=True),
            lax.all_gather(up_shift, "fsdp", axis=0, tiled=True),
            lax.all_gather(down_matrix, "fsdp", axis=0, tiled=True),
            lax.all_gather(down_shift, "fsdp", axis=0, tiled=True),
        )
        output_rows, stored = run_forward(tokens[lower:upper], tissue[lower:upper], forward_weights)
        output_list.append(output_rows)
        backward_weights = (
            lax.all_gather(norm1_gain, "fsdp", axis=0, tiled=True),
            lax.all_gather(norm1_shift, "fsdp", axis=0, tiled=True),
            lax.all_gather(qkv_matrix, "fsdp", axis=0, tiled=True),
            lax.all_gather(qkv_shift, "fsdp", axis=0, tiled=True),
            lax.all_gather(proj_matrix, "fsdp", axis=0, tiled=True),
            lax.all_gather(proj_shift, "fsdp", axis=0, tiled=True),
            lax.all_gather(norm2_gain, "fsdp", axis=0, tiled=True),
            lax.all_gather(norm2_shift, "fsdp", axis=0, tiled=True),
            lax.all_gather(up_matrix, "fsdp", axis=0, tiled=True),
            lax.all_gather(up_shift, "fsdp", axis=0, tiled=True),
            lax.all_gather(down_matrix, "fsdp", axis=0, tiled=True),
            lax.all_gather(down_shift, "fsdp", axis=0, tiled=True),
        )
        grad_input, gradients = run_backward(cotangent[lower:upper], stored, backward_weights)
        grad_list.append(grad_input)
        shares = (
            lax.psum_scatter(
                gradients[0].astype(jnp.bfloat16), "fsdp", scatter_dimension=0, tiled=True
            ).astype(jnp.float32),
            lax.psum_scatter(
                gradients[1].astype(jnp.bfloat16), "fsdp", scatter_dimension=0, tiled=True
            ).astype(jnp.float32),
            lax.psum_scatter(
                gradients[2].astype(jnp.bfloat16), "fsdp", scatter_dimension=0, tiled=True
            ).astype(jnp.float32),
            lax.psum_scatter(
                gradients[3].astype(jnp.bfloat16), "fsdp", scatter_dimension=0, tiled=True
            ).astype(jnp.float32),
            lax.psum_scatter(
                gradients[4].astype(jnp.bfloat16), "fsdp", scatter_dimension=0, tiled=True
            ).astype(jnp.float32),
            lax.psum_scatter(
                gradients[5].astype(jnp.bfloat16), "fsdp", scatter_dimension=0, tiled=True
            ).astype(jnp.float32),
            lax.psum_scatter(
                gradients[6].astype(jnp.bfloat16), "fsdp", scatter_dimension=0, tiled=True
            ).astype(jnp.float32),
            lax.psum_scatter(
                gradients[7].astype(jnp.bfloat16), "fsdp", scatter_dimension=0, tiled=True
            ).astype(jnp.float32),
            lax.psum_scatter(
                gradients[8].astype(jnp.bfloat16), "fsdp", scatter_dimension=0, tiled=True
            ).astype(jnp.float32),
            lax.psum_scatter(
                gradients[9].astype(jnp.bfloat16), "fsdp", scatter_dimension=0, tiled=True
            ).astype(jnp.float32),
            lax.psum_scatter(
                gradients[10].astype(jnp.bfloat16), "fsdp", scatter_dimension=0, tiled=True
            ).astype(jnp.float32),
            lax.psum_scatter(
                gradients[11].astype(jnp.bfloat16), "fsdp", scatter_dimension=0, tiled=True
            ).astype(jnp.float32),
        )
        owned = shares if owned is None else add_trees(owned, shares)
    totals = (
        lax.psum(owned[0].astype(jnp.bfloat16), "dp").astype(jnp.float32),
        lax.psum(owned[1].astype(jnp.bfloat16), "dp").astype(jnp.float32),
        lax.psum(owned[2].astype(jnp.bfloat16), "dp").astype(jnp.float32),
        lax.psum(owned[3].astype(jnp.bfloat16), "dp").astype(jnp.float32),
        lax.psum(owned[4].astype(jnp.bfloat16), "dp").astype(jnp.float32),
        lax.psum(owned[5].astype(jnp.bfloat16), "dp").astype(jnp.float32),
        lax.psum(owned[6].astype(jnp.bfloat16), "dp").astype(jnp.float32),
        lax.psum(owned[7].astype(jnp.bfloat16), "dp").astype(jnp.float32),
        lax.psum(owned[8].astype(jnp.bfloat16), "dp").astype(jnp.float32),
        lax.psum(owned[9].astype(jnp.bfloat16), "dp").astype(jnp.float32),
        lax.psum(owned[10].astype(jnp.bfloat16), "dp").astype(jnp.float32),
        lax.psum(owned[11].astype(jnp.bfloat16), "dp").astype(jnp.float32),
    )
    out_tokens = jnp.concatenate(output_list, axis=0)
    tokens_grad = jnp.concatenate(grad_list, axis=0)
    return (
        out_tokens,
        tokens_grad,
        totals[0],
        totals[1],
        totals[2],
        totals[3],
        totals[4],
        totals[5],
        totals[6],
        totals[7],
        totals[8],
        totals[9],
        totals[10],
        totals[11],
    )


def solution(mesh):
    in_specs = (
        P(("dp", "fsdp"), None, None),
        P(("dp", "fsdp"), None),
        P("fsdp"),
        P("fsdp"),
        P("fsdp", None),
        P("fsdp"),
        P("fsdp", None),
        P("fsdp"),
        P("fsdp"),
        P("fsdp"),
        P("fsdp", None),
        P("fsdp"),
        P("fsdp", None),
        P("fsdp"),
        P(("dp", "fsdp"), None, None),
    )
    out_specs = (
        P(("dp", "fsdp"), None, None),
        P(("dp", "fsdp"), None, None),
        P("fsdp"),
        P("fsdp"),
        P("fsdp", None),
        P("fsdp"),
        P("fsdp", None),
        P("fsdp"),
        P("fsdp"),
        P("fsdp"),
        P("fsdp", None),
        P("fsdp"),
        P("fsdp", None),
        P("fsdp"),
    )
    return jax.shard_map(
        on_device, mesh=mesh, in_specs=in_specs, out_specs=out_specs, check_vma=False
    )
```

profile of v0, /device:TPU:0, one launch (start us, length us, event | category | flops | bytes accessed | tf_op | source)
XLA Modules:
  0.0 672.4 jit_solution(15701481505306696767)
XLA Ops:
  34.1 7.3 %add_convert_fusion.3 = bf16[4,196,2304]{2,1,0:T(8,128)(2,1)} fusion(f32[2304]{0:T(1024)S(1)} %pad_maximum_fusion.2, bf16[768,2304]{1,0:T(8,128)(2,1)} %all-gather.13.cloned.1.call-done, f32[768]{0:T(1024)S(1)} %reshape.231, f32[768]{0:T(1024)S(1)} %reshape.230, f32[4,196]{1,0:T(4,128)S(1)} %fusion.98, f32[4,196]{1,0:T(4,128)S(1)} %broadcast_multiply_fusion.3, ...), kind=kOutput, calls=%fused_computation.60 | convolution fusion | flops 2781757440 | bytes 8377472 | tf_op jit(solution)/shard_map/bpd,de->bpe/dot_general | solution.py:31
  71.9 6.7 copy.97
  93.5 11.2 %fusion.26 = f32[4,196,3072]{2,1,0:T(8,128)} fusion(bf16[768,3072]{1,0:T(8,128)(2,1)} %all-gather.17.cloned.1.call-done, f32[4,196,768]{2,1,0:T(8,128)} %copy-done.19, f32[4,196]{1,0:T(4,128)S(1)} %fusion.101, f32[4,196]{1,0:T(4,128)S(1)} %broadcast_multiply_fusion, f32[768]{0:T(1024)S(1)} %reshape.234, f32[768]{0:T(1024)S(1)} %reshape.233), kind=kOutput, calls=%fused_computation.75 | convolution fusion | flops 3702386688 | bytes 16773248 | tf_op jit(solution)/shard_map/bpd,de->bpe/dot_general | solution.py:31
  104.7 19.9 %fusion.62 = (u8[196,3072]{1,0:T(8,128)(4,1)S(1)}, u8[196,3072]{1,0:T(8,128)(4,1)S(1)}, u8[196,3072]{1,0:T(8,128)(4,1)S(1)}, u8[196,3072]{1,0:T(8,128)(4,1)S(1)}, f32[4,196,3072]{2,1,0:T(8,128)}) fusion(f32[3072]{0:T(1024)S(1)} %bitcast.200, f32[4,196,3072]{2,1,0:T(8,128)} %fusion.26, bf16[768,3072]{1,0:T(8,128)(2,1)} %all-gather.17.cloned.1.call-done, ...), kind=kOutput, calls=%fused_computation.148 | convolution fusion | flops 3767414784 | bytes 28827776 | tf_op jit(solution)/shard_map/bpd,de->bpe/dot_general | solution.py:31
  124.7 50.1 %multiply_convert_fusion.3 = (bf16[4,196,3072]{2,1,0:T(8,128)(2,1)}, f32[4,196,3072]{2,1,0:T(8,128)}, bf16[4,196,3072]{2,1,0:T(8,128)(2,1)}, f32[4,196,3072]{2,1,0:T(8,128)}) fusion(f32[4,196,3072]{2,1,0:T(8,128)} %get-tuple-element.157, f32[3072]{0:T(1024)S(1)} %bitcast.201, u8[196,3072]{1,0:T(8,128)(4,1)S(1)} %get-tuple-element.57, ...), kind=kLoop, calls=%fused_computation.35 | loop fusion | flops 339591168 | bytes 50589696 | tf_op jit(solution)/shard_map/convert_element_type | solution.py:107
  174.8 13.8 %fusion.129 = (bf16[3072]{0:T(1024)(128)(2,1)}, bf16[4,196,3072]{2,1,0:T(8,128)(2,1)}) fusion(f32[4,196,3072]{2,1,0:T(8,128)} %get-tuple-element.133, bf16[3072,768]{1,0:T(8,128)(2,1)} %all-gather.19.cloned.1.call-done, bf16[4,196,768]{2,0,1:T(4,128)(2,1)S(1)} %copy-done.12, f32[4,196,3072]{2,1,0:T(8,128)} %fusion.26, f32[3072]{0:T(1024)S(1)} %bitcast.202), kind=kOutput, calls=%fused_computation.253 | convolution fusion | flops 3737908224 | bytes 30025728 | tf_op jit(solution)/shard_map/bpe,de->bpd/dot_general | solution.py:35
  188.6 9.4 %fusion.22 = f32[4,196,768]{2,1,0:T(8,128)} fusion(bf16[4,196,3072]{2,1,0:T(8,128)(2,1)} %get-tuple-element.165, bf16[768,3072]{1,0:T(8,128)(2,1)} %all-gather.17.cloned.1.call-done), kind=kOutput, calls=%fused_computation.71 | convolution fusion | flops 3699376128 | bytes 11943936 | tf_op jit(solution)/shard_map/bpe,de->bpd/dot_general | solution.py:35
  198.1 13.1 %fusion.130 = (bf16[3072]{0:T(1024)(128)(2,1)}, bf16[4,196,3072]{2,1,0:T(8,128)(2,1)}) fusion(f32[4,196,3072]{2,1,0:T(8,128)} %get-tuple-element.121, bf16[3072,768]{1,0:T(8,128)(2,1)} %all-gather.19.cloned.1.call-done, bf16[4,196,768]{2,0,1:T(4,128)(2,1)S(1)} %copy-done.11, f32[4,196,3072]{2,1,0:T(8,128)S(1)} %copy-done.13, f32[3072]{0:T(1024)S(1)} %bitcast.203), kind=kOutput, calls=%fused_computation.254 | convolution fusion | flops 3737908224 | bytes 30025728 | tf_op jit(solution)/shard_map/bpe,de->bpd/dot_general | solution.py:35
  211.2 10.6 %multiply_reduce_fusion.3 = (bf16[768]{0:T(1024)(128)(2,1)}, f32[4,196]{1,0:T(4,128)S(1)}, bf16[768]{0:T(1024)(128)(2,1)}, bf16[768]{0:T(1024)(128)(2,1)}, f32[4...) fusion(f32[4,196,768]{2,1,0:T(8,128)S(1)} %copy-done.16, f32[4,196]{1,0:T(4,128)S(1)} %fusion.99, ...), kind=kOutput, calls=%fused_computation.133 | convolution fusion | flops 3709005312 | bytes 19197312 | tf_op jit(solution)/shard_map/bpe,de->bpd/dot_general | solution.py:35
  237.9 10.1 %multiply_reduce_fusion.1 = (f32[4,12,196]{2,1,0:T(8,128)S(1)}, f32[4,12,196,196]{2,3,1,0:T(8,128)}) fusion(f32[4,12,196,196]{2,3,1,0:T(8,128)} %copy-done.1, f32[4,12,196]{2,1,0:T(8,128)S(1)} %log_add_fusion.1, pred[4,196]{1,0:T(4,128)(4,1)S(1)} %get-tuple-element.134, bf16[4,196,3,12,64]{1,4,3,2,0:T(8,128)(2,1)} %bitcast.187, ...), kind=kOutput, calls=%fused_computation.17 | convolution fusion | flops 246442560 | bytes 21266768 | tf_op jit(solution)/shard_map/bqhd,bkhd->bhqk/dot_general | solution.py:178
  248.0 11.8 %multiply_convert_fusion.1 = bf16[4,12,196,196]{2,3,1,0:T(8,128)(2,1)} fusion(f32[4,12,196,196]{2,3,1,0:T(8,128)} %get-tuple-element.160, f32[4,12,196,196]{2,3,1,0:T(8,128)} %copy-done.1, f32[4,12,196]{2,1,0:T(8,128)S(1)} %get-tuple-element.159, f32[4,12,196]{2,1,0:T(8,128)S(1)} %log_add_fusion.1, pred[4,196]{1,0:T(4,128)(4,1)S(1)} %get-tuple-element.134), kind=kLoop, calls=%fused_computation.16 | loop fusion | flops 11063808 | bytes 18515728 | tf_op jit(solution)/shard_map/convert_element_type | solution.py:188
  269.5 6.5 convolution_bitcast_fusion.1
  290.4 11.2 %multiply_reduce_fusion = (f32[4,12,196]{2,1,0:T(8,128)S(1)}, f32[4,12,196,196]{2,3,1,0:T(8,128)}) fusion(f32[4,12,196,196]{2,3,1,0:T(8,128)} %copy-done, f32[4,12,196]{2,1,0:T(8,128)S(1)} %log_add_fusion, pred[4,196]{1,0:T(4,128)(4,1)S(1)} %get-tuple-element.135, bf16[4,196,3,12,64]{1,4,3,2,0:T(8,128)(2,1)} %bitcast.182, ...), kind=kOutput, calls=%fused_computation.14 | convolution fusion | flops 246442560 | bytes 21266768 | tf_op jit(solution)/shard_map/bqhd,bkhd->bhqk/dot_general | solution.py:178
  301.6 12.2 %multiply_convert_fusion = bf16[4,12,196,196]{2,3,1,0:T(8,128)(2,1)} fusion(f32[4,12,196,196]{2,3,1,0:T(8,128)} %get-tuple-element.162, f32[4,12,196,196]{2,3,1,0:T(8,128)} %copy-done, f32[4,12,196]{2,1,0:T(8,128)S(1)} %get-tuple-element.161, f32[4,12,196]{2,1,0:T(8,128)S(1)} %log_add_fusion, pred[4,196]{1,0:T(4,128)(4,1)S(1)} %get-tuple-element.135), kind=kLoop, calls=%fused_computation.13 | loop fusion | flops 11063808 | bytes 18515728 | tf_op jit(solution)/shard_map/convert_element_type | solution.py:188
  337.8 9.8 %bitcast_convert_fusion.3 = bf16[768,3072]{1,0:T(8,128)(2,1)} fusion(bf16[4,196,3072]{2,1,0:T(8,128)(2,1)} %get-tuple-element.167, f32[4,196,768]{2,1,0:T(8,128)} %copy-done.14, f32[768]{0:T(1024)S(1)} %reshape.234, f32[768]{0:T(1024)S(1)} %reshape.233, f32[4,196]{1,0:T(4,128)S(1)} %fusion.99, f32[4,196]{1,0:T(4,128)S(1)} %broadcast_multiply_fusion.2), kind=kOutput, calls=%fused_computation.56 | convolution fusion | flops 3704745984 | bytes 11956352 | tf_op jit(solution)/shard_map/bpd,bpe->de/dot_general | solution.py:39
  347.7 10.1 %bitcast_convert_fusion.2 = bf16[768,3072]{1,0:T(8,128)(2,1)} fusion(bf16[4,196,3072]{2,1,0:T(8,128)(2,1)} %get-tuple-element.165, f32[4,196,768]{2,1,0:T(8,128)} %copy-done.19, f32[4,196]{1,0:T(4,128)S(1)} %fusion.101, f32[4,196]{1,0:T(4,128)S(1)} %broadcast_multiply_fusion, f32[768]{0:T(1024)S(1)} %reshape.234, f32[768]{0:T(1024)S(1)} %reshape.233), kind=kOutput, calls=%fused_computation.55 | convolution fusion | flops 3704745984 | bytes 11956352 | tf_op jit(solution)/shard_map/bpd,bpe->de/dot_general | solution.py:39
  357.9 8.8 %bitcast_convert_fusion.1 = bf16[3072,768]{1,0:T(8,128)(2,1)} fusion(bf16[4,196,3072]{2,1,0:T(8,128)(2,1)} %get-tuple-element.120, bf16[4,196,768]{2,0,1:T(4,128)(2,1)} %get-tuple-element.124), kind=kOutput, calls=%fused_computation.54 | convolution fusion | flops 3701735424 | bytes 10739712 | tf_op jit(solution)/shard_map/bpd,bpe->de/dot_general | solution.py:39
  366.8 9.0 %bitcast_convert_fusion = bf16[3072,768]{1,0:T(8,128)(2,1)} fusion(bf16[4,196,3072]{2,1,0:T(8,128)(2,1)} %get-tuple-element.132, bf16[4,196,768]{2,0,1:T(4,128)(2,1)} %get-tuple-element.125), kind=kOutput, calls=%fused_computation.53 | convolution fusion | flops 3701735424 | bytes 10739712 | tf_op jit(solution)/shard_map/bpd,bpe->de/dot_general | solution.py:39
  381.3 9.2 %fusion.38 = f32[4,196,768]{2,1,0:T(8,128)} fusion(bf16[4,196,2304]{1,2,0:T(8,128)(2,1)} %bitcast.199, bf16[768,2304]{1,0:T(8,128)(2,1)} %all-gather.13.cloned.1.call-done), kind=kOutput, calls=%fused_computation.99 | convolution fusion | flops 2774532096 | bytes 9560064 | tf_op jit(solution)/shard_map/bpe,de->bpd/dot_general | solution.py:35
  402.2 14.1 %reduce-scatter.23.cloned.1.call-done = bf16[1536,768]{1,0:T(8,128)(2,1)} async-done(((bf16[3072,768]{1,0:T(8,128)(2,1)}), bf16[1536,768]{1,0:T(8,128)(2,1)}) %reduce-scatter.23.cloned.1.call-update) | async-done | bytes 2359312 | tf_op jit(solution)/shard_map/reduce_scatter | solution.py:316
  420.6 8.9 %fusion.112 = (bf16[768]{0:T(1024)(128)(2,1)S(1)}, f32[4,196]{1,0:T(4,128)S(1)}, f32[4,196]{1,0:T(4,128)S(1)}, bf16[768]{0:T(1024)(128)(2,1)S(1)}, f32[4,196,768]{2,1,0:T(8,128)S(1)}) fusion(f32[768]{0:T(1024)S(1)} %reshape.230, f32[4,196]{1,0:T(4,128)S(1)} %copy-done.35, bf16[4,196,768]{2,0,1:T(4,128)(2,1)S(1)} %copy-done.4, f32[4,196,768]{2,1,0:T(8,128)} %fusion.38, ...), kind=kOutput, calls=%fused_computation.240 | convolution fusion | flops 2781754368 | bytes 14395648 | tf_op jit(solution)/shard_map/bpe,de->bpd/dot_general | solution.py:35
  436.9 80.4 %all-reduce.16 = (bf16[384]{0:T(512)(128)(2,1)S(1)}, bf16[384]{0:T(512)(128)(2,1)S(1)}, bf16[768]{0:T(1024)(128)(2,1)S(1)}, bf16[384]{0:T(512)(128)(2,1)S(1)}, b...) all-reduce(bf16[384]{0:T(512)(128)(2,1)S(1)} %add_convert_fusion.25, ...), channel_id=1, replica_groups=mesh['dp'=16,'fsdp'=2] {'dp'}, use_global_device_ids=true, to_apply=%region_26.27 | all-reduce | flops 4608 | bytes 18432 | tf_op jit(solution)/shard_map/psum | solution.py:325
  530.8 8.0 %add_convert_fusion.11 = bf16[4,196,768]{2,1,0:T(8,128)(2,1)S(1)} fusion(f32[4,196,768]{2,1,0:T(8,128)S(1)} %copy-done.18, bf16[4,196,3072]{2,1,0:T(8,128)(2,1)} %get-tuple-element.120, bf16[3072,768]{1,0:T(8,128)(2,1)} %all-gather.19.cloned.1.call-done, f32[768]{0:T(1024)S(1)} %reshape.236), kind=kOutput, calls=%fused_computation.143 | convolution fusion | flops 3701182464 | bytes 13151232 | tf_op jit(solution)/shard_map/bpd,de->bpe/dot_general | solution.py:31
  545.0 110.2 %all-reduce.21.cloned.1.call-done = (bf16[384,2304]{1,0:T(8,128)(2,1)}, bf16[384,768]{1,0:T(8,128)(2,1)}, bf16[384,3072]{1,0:T(8,128)(2,1)}, bf16[1536,768]{1,0:T(8,128)(2,1)}) async-done(((bf16[384,2304]{1,0:T(8,128)(2,1)}, bf16[384,768]{1,0:T(8,128)(2,1)}, bf16[384,3072]{1,0:T(8,128)(2,1)}, bf16[1536,768]{1,0:T(8,128)(2,1)}), (bf16[384,2304]{1,0:T(8,128)(2,1)}, bf16[384,768]{1,0:T(8,128)(2,1)}, ...) | async-done | bytes 7077904 | tf_op jit(solution)/shard_map/psum | solution.py:327
  (313 shorter events, 192.3 us)
Async XLA Ops:
  7.2 26.9 %all-gather.13.cloned.1.call-start = ((), (), s32[]{:S(2)}) async-start(), calls=%async_computation.8 | async-start | bytes 5308416 | tf_op jit(solution)/shard_map/all_gather | solution.py:256
  7.9 53.5 %all-gather.15.cloned.1.call-start = ((), (), s32[]{:S(2)}) async-start(), calls=%async_computation.9 | async-start | bytes 1769472 | tf_op jit(solution)/shard_map/all_gather | solution.py:258
  8.7 84.8 %all-gather.17.cloned.1.call-start = ((), (), s32[]{:S(2)}) async-start(), calls=%async_computation.10 | async-start | bytes 7077888 | tf_op jit(solution)/shard_map/all_gather | solution.py:262
  9.4 165.4 %all-gather.19.cloned.1.call-start = ((), (), s32[]{:S(2)}) async-start(), calls=%async_computation.11 | async-start | bytes 7077888 | tf_op jit(solution)/shard_map/all_gather | solution.py:264
  10.0 380.6 %reduce-scatter.13.cloned.1.call-start = ((), (), s32[]{:S(2)}) async-start(), calls=%async_computation.14 | async-start | bytes 1769472 | tf_op jit(solution)/shard_map/reduce_scatter | solution.py:298
  13.5 48.0 %copy-start.3 = (bf16[4,196,768]{2,0,1:T(4,128)(2,1)}, bf16[4,196,768]{2,0,1:T(4,128)(2,1)S(1)}, u32[]{:S(2)}) copy-start(bf16[4,196,768]{2,0,1:T(4,128)(2,1)S(1)} %get-tuple-element.126) | copy-start | bytes 3612676
  13.5 77.2 %copy-start.5 = (bf16[4,196,768]{2,0,1:T(4,128)(2,1)}, bf16[4,196,768]{2,0,1:T(4,128)(2,1)S(1)}, u32[]{:S(2)}) copy-start(bf16[4,196,768]{2,0,1:T(4,128)(2,1)S(1)} %get-tuple-element.127) | copy-start | bytes 3612676
  13.5 12.7 %copy-start.51 = (bf16[1536]{0:T(1024)(128)(2,1)S(1)}, bf16[1536]{0:T(1024)(128)(2,1)}, u32[]{:S(2)}) copy-start(bf16[1536]{0:T(1024)(128)(2,1)} %param.26) | copy-start | bytes 9220
  13.9 20.1 %copy-start.34 = (f32[4,196]{1,0:T(4,128)}, f32[4,196]{1,0:T(4,128)S(1)}, u32[]{:S(2)}) copy-start(f32[4,196]{1,0:T(4,128)S(1)} %broadcast_multiply_fusion.3) | copy-start | bytes 9412
  14.4 11.7 %copy-start.42 = (f32[4,196]{1,0:T(4,128)}, f32[4,196]{1,0:T(4,128)S(1)}, u32[]{:S(2)}) copy-start(f32[4,196]{1,0:T(4,128)S(1)} %fusion.54) | copy-start | bytes 9412
  14.5 26.9 %copy-start.38 = (f32[4,196]{1,0:T(4,128)}, f32[4,196]{1,0:T(4,128)S(1)}, u32[]{:S(2)}) copy-start(f32[4,196]{1,0:T(4,128)S(1)} %fusion.98) | copy-start | bytes 9412
  22.0 45.0 %copy-start.36 = (f32[4,196]{1,0:T(4,128)}, f32[4,196]{1,0:T(4,128)S(1)}, u32[]{:S(2)}) copy-start(f32[4,196]{1,0:T(4,128)S(1)} %broadcast_multiply_fusion.1) | copy-start | bytes 9412
  22.5 44.5 %copy-start.40 = (f32[4,196]{1,0:T(4,128)}, f32[4,196]{1,0:T(4,128)S(1)}, u32[]{:S(2)}) copy-start(f32[4,196]{1,0:T(4,128)S(1)} %fusion.100) | copy-start | bytes 9412
  124.7 50.1 %copy-start.12 = (bf16[4,196,768]{2,0,1:T(4,128)(2,1)S(1)}, bf16[4,196,768]{2,0,1:T(4,128)(2,1)}, u32[]{:S(2)}) copy-start(bf16[4,196,768]{2,0,1:T(4,128)(2,1)} %get-tuple-element.125) | copy-start | bytes 3612676
  198.0 13.1 %copy-start.16 = (f32[4,196,768]{2,1,0:T(8,128)S(1)}, f32[4,196,768]{2,1,0:T(8,128)}, u32[]{:S(2)}) copy-start(f32[4,196,768]{2,1,0:T(8,128)} %copy-done.14) | copy-start | bytes 7225348
  229.2 161.3 %reduce-scatter.15.cloned.1.call-start = ((), (), s32[]{:S(2)}) async-start(), calls=%async_computation.15 | async-start | bytes 1769472 | tf_op jit(solution)/shard_map/reduce_scatter | solution.py:298
  264.9 127.9 %reduce-scatter.9.cloned.1.call-start = ((), (), s32[]{:S(2)}) async-start(), calls=%async_computation.12 | async-start | bytes 5308416 | tf_op jit(solution)/shard_map/reduce_scatter | solution.py:292
  286.4 106.4 %reduce-scatter.11.cloned.1.call-start = ((), (), s32[]{:S(2)}) async-start(), calls=%async_computation.13 | async-start | bytes 5308416 | tf_op jit(solution)/shard_map/reduce_scatter | solution.py:292
  337.7 59.3 %reduce-scatter.17.cloned.1.call-start = ((), (), s32[]{:S(2)}) async-start(), calls=%async_computation.16 | async-start | bytes 7077888 | tf_op jit(solution)/shard_map/reduce_scatter | solution.py:310
  347.6 49.4 %reduce-scatter.19.cloned.1.call-start = ((), (), s32[]{:S(2)}) async-start(), calls=%async_computation.17 | async-start | bytes 7077888 | tf_op jit(solution)/shard_map/reduce_scatter | solution.py:310
  357.8 44.3 %reduce-scatter.21.cloned.1.call-start = ((), (), s32[]{:S(2)}) async-start(), calls=%async_computation.18 | async-start | bytes 7077888 | tf_op jit(solution)/shard_map/reduce_scatter | solution.py:316
  366.7 49.5 %reduce-scatter.23.cloned.1.call-start = ((), (), s32[]{:S(2)}) async-start(), calls=%async_computation.19 | async-start | bytes 7077888 | tf_op jit(solution)/shard_map/reduce_scatter | solution.py:316
  375.8 279.5 %all-reduce.21.cloned.1.call-start = ((), (), s32[]{:S(2)}) async-start(), calls=%async_computation.20 | async-start | bytes 14155776 | tf_op jit(solution)/shard_map/psum | solution.py:327
  522.0 16.8 %slice-start = ((s8[4915200]{0:T(1024)(128)(4,1)}), s8[4194304]{0:T(1024)(128)(4,1)S(1)}, s32[]{:S(2)}) async-start(s8[4915200]{0:T(1024)(128)(4,1)} %bitcast.194), calls=%async_computation.21 | async-start | bytes 8388608
  (62 other events, 303.6 us)
Sparse Core Ops, SparseCore 0:
  9.6 15.3 all-gather.12
  26.6 10.3 all-gather.14
  38.5 15.5 all-gather.16
  55.6 15.6 all-gather.18
  229.4 10.7 reduce-scatter.12
  265.0 10.7 reduce-scatter.14
  286.5 13.5 reduce-scatter.8
  337.8 13.9 reduce-scatter.10
  354.1 13.7 reduce-scatter.16
  370.2 13.7 reduce-scatter.18
  386.3 13.7 reduce-scatter.20
  402.4 13.7 reduce-scatter.22
  423.8 231.3 all-reduce.20
where the time goes:
time: 677 us; the launch traced here: 672 us
  matrix products  255 us (38%)
  other arithmetic  135 us (20%)
  waiting for transfers between devices  127 us (19%)
  blocking collectives  98.9 us (15%)
  local copies, waits for them, and re-layouts  37.7 us (6%)
  between operations  17.5 us (3%)
    psum x1, waiting for transfers between devices, on_device(): lax.psum(owned[2].astype(jnp.bfloat16), 'dp').astype(jnp.float32)  110 us
    psum x1, blocking collectives, on_device(): lax.psum(owned[0].astype(jnp.bfloat16), 'dp').astype(jnp.float32)  80.4 us
    dot_general x8, matrix products, product_back(): jnp.einsum('bpe,de->bpd', rows_in, matrix, preferred_element_type=jnp.flo...  70.9 us
    dot_general x8, matrix products, product(): jnp.einsum('bpd,de->bpe', rows_in, matrix, preferred_element_type=jnp.flo...  60.2 us
    dot_general x8, matrix products, outer_sum(): jnp.einsum('bpd,bpe->de', left_rows, right_rows, preferred_element_type=j...  55.2 us
    convert_element_type x1, other arithmetic, run_forward(): active = active_float.astype(jnp.bfloat16)  50.1 us
    convert_element_type x2, other arithmetic, run_backward(): grad_scores = (softmax * (grad_probs - row_dot)).astype(jnp.bfloat16)  24 us
    dot_general x2, matrix products, run_backward(): jnp.einsum('bqhd,bkhd->bhqk', grad_mixed, value_rows, preferred_element_t...  21.3 us
  transfers between devices with their start and end apart: 13, of which 2 were waited for; matrix products, arithmetic and copies ran while one was open for 52% of the time, Pallas kernels for 0%

commit v1 on v0

v1 whole, which is shorter than its diff:
```python
import functools

import jax
import jax.numpy as jnp
from jax import lax
from jax.experimental import pallas as pl
from jax.experimental.pallas import tpu as pltpu
from jax.sharding import PartitionSpec as P

HEADS = 12
EPS = 1e-06
BF = jnp.bfloat16
F32 = jnp.float32
MESH = pl.DeviceIdType.MESH
ERF = (0.254829592, -0.284496736, 1.421413741, -1.453152027, 1.061405429)


def dot(a, b, ca, cb):
    return lax.dot_general(a, b, (((ca,), (cb,)), ((), ())), preferred_element_type=F32)


def aligned(start, size, step):
    if isinstance(start, int):
        return pl.ds(start, size)
    return pl.ds(pl.multiple_of(start, step), size)


def gelu_both(h):
    t = 1.0 / (1.0 + (0.3275911 * 0.7071067811865476) * jnp.abs(h))
    e = jnp.exp(-0.5 * h * h)
    tail = t * (ERF[0] + t * (ERF[1] + t * (ERF[2] + t * (ERF[3] + t * ERF[4])))) * (0.5 * e)
    cdf = jnp.where(h >= 0, 1.0 - tail, tail)
    return h * cdf, cdf + h * e * 0.3989422804014327


def normalized(v):
    mean = jnp.mean(v, axis=-1, keepdims=True)
    centred = v - mean
    var = jnp.mean(centred * centred, axis=-1, keepdims=True)
    rstd = lax.rsqrt(var + EPS)
    return centred * rstd, rstd


def head_masks(scale):
    lane = lax.broadcasted_iota(jnp.int32, (1, 128), 1)
    return [
        jnp.where(lane < 64, scale, 0.0).astype(BF),
        jnp.where(lane >= 64, scale, 0.0).astype(BF),
    ]


def front_kernel(
    x_hbm, cot_hbm, tissue, g1, b1, qkv_w_hbm, qkv_b, proj_w_hbm, proj_b, g2, b2,
    xp_o, cotp_o, first_o, qkv_o, pt_o, ho_o, res_o, s2_o, tb_o,
    x3, cot3, xp, cotp, first, qkv_w, qkv, pt, ho, proj_w, res, s2, tb, sem, osem, psem,
):
    images, slots, width = x3.shape
    padded = xp.shape[0] // images
    scores_w = pt.shape[-1]

    loads = {
        "x": pltpu.make_async_copy(x_hbm, x3, sem.at[0]),
        "qkv_w": pltpu.make_async_copy(qkv_w_hbm, qkv_w, sem.at[1]),
        "proj_w": pltpu.make_async_copy(proj_w_hbm, proj_w, sem.at[2]),
        "cot": pltpu.make_async_copy(cot_hbm, cot3, sem.at[3]),
    }
    for copy in loads.values():
        copy.start()
    stores = []

    def store(n, src, dst):
        copy = pltpu.make_async_copy(src, dst, osem.at[n])
        copy.start()
        stores.append(copy)

    pad_rows = jnp.zeros((padded - slots, width), BF)
    loads["x"].wait()

    @pl.loop(0, images)
    def _(i):
        rows = aligned(i * padded, padded, 16)
        block = jnp.concatenate([x3[i], pad_rows], axis=0)
        xp[rows] = block
        n, _ = normalized(block.astype(F32))
        first[rows] = (n * g1[...] + b1[...]).astype(BF)
        t_row = jnp.concatenate(
            [tissue[i].astype(F32), jnp.zeros((1, padded - slots), F32)], axis=1
        )
        tb[i] = jnp.broadcast_to(t_row, (128, padded)).T

    store(0, xp, xp_o)
    store(1, first, first_o)
    store(2, tb, tb_o)
    loads["qkv_w"].wait()
    for part in range(3):
        cols = slice(part * width, (part + 1) * width)
        prod = dot(first[...], qkv_w[:, cols], 1, 0)
        if part == 0:
            prod = prod + qkv_b[:, :width]
        if part == 2:
            prod = prod + qkv_b[:, width:]
        qkv[:, cols] = prod.astype(BF)
    store(3, qkv, qkv_o)

    scaled = head_masks(0.125)
    ones = head_masks(1.0)

    @pl.loop(0, images)
    def _(i):
        rows = aligned(i * padded, padded, 16)
        slot = lax.rem(i, 2)
        out = pltpu.make_async_copy(pt.at[slot], pt_o.at[i], psem.at[slot])

        @pl.when(i >= 2)
        def _():
            out.wait()

        t = tb[i]
        valid = jnp.concatenate([t, t[:, : scores_w - 128]], axis=1) > 0
        for pair in range(HEADS // 2):
            cols = [slice(b * width + pair * 128, b * width + pair * 128 + 128) for b in range(3)]
            q, k, v = qkv[rows, cols[0]], qkv[rows, cols[1]], qkv[rows, cols[2]]
            mixed = None
            for h in range(2):
                st = jnp.where(valid, dot(k * scaled[h], q, 1, 1), -1e30)
                e = jnp.exp(st - jnp.max(st, axis=0, keepdims=True))
                probs = (e * (1.0 / jnp.sum(e, axis=0, keepdims=True))).astype(BF)
                pt[slot, pair * 2 + h] = probs
                part = dot(probs, v * ones[h], 0, 0)
                mixed = part if mixed is None else mixed + part
            ho[rows, cols[0]] = (mixed * t).astype(BF)
        out.start()

    store(4, ho, ho_o)
    loads["proj_w"].wait()
    res[...] = dot(ho[...], proj_w[...], 1, 0)

    @pl.loop(0, images)
    def _(i):
        rows = aligned(i * padded, padded, 16)
        total = xp[rows].astype(F32) + res[rows] + proj_b[...]
        res[rows] = total
        n, _ = normalized(total)
        s2[rows] = (n * g2[...] + b2[...]).astype(BF)

    store(5, s2, s2_o)
    store(6, res, res_o)
    loads["cot"].wait()

    @pl.loop(0, images)
    def _(i):
        cotp[aligned(i * padded, padded, 16)] = jnp.concatenate([cot3[i], pad_rows], axis=0)

    store(7, cotp, cotp_o)
    for slot in range(2):
        pltpu.make_async_copy(pt.at[slot], pt_o.at[0], psem.at[slot]).wait()
    for copy in stores:
        copy.wait()


def front(tokens, cot, tissue, vec, qkv_w, proj_w):
    images, slots, width = tokens.shape
    padded = -(-slots // 16) * 16
    rows = images * padded
    vm = pl.BlockSpec(memory_space=pltpu.VMEM)
    hbm = pl.BlockSpec(memory_space=pl.ANY)
    sds = jax.ShapeDtypeStruct
    return pl.pallas_call(
        front_kernel,
        out_shape=[
            sds((rows, width), BF),
            sds((rows, width), BF),
            sds((rows, width), BF),
            sds((rows, 3 * width), BF),
            sds((images, HEADS, padded, padded), BF),
            sds((rows, width), BF),
            sds((rows, width), F32),
            sds((rows, width), BF),
            sds((images, padded, 128), F32),
        ],
        in_specs=[hbm, hbm, vm, vm, vm, hbm, vm, hbm, vm, vm, vm],
        out_specs=[hbm] * 9,
        scratch_shapes=[
            pltpu.VMEM((images, slots, width), BF),
            pltpu.VMEM((images, slots, width), BF),
            pltpu.VMEM((rows, width), BF),
            pltpu.VMEM((rows, width), BF),
            pltpu.VMEM((rows, width), BF),
            pltpu.VMEM((width, 3 * width), BF),
            pltpu.VMEM((rows, 3 * width), BF),
            pltpu.VMEM((2, HEADS, padded, padded), BF),
            pltpu.VMEM((rows, width), BF),
            pltpu.VMEM((width, width), BF),
            pltpu.VMEM((rows, width), F32),
            pltpu.VMEM((rows, width), BF),
            pltpu.VMEM((images, padded, 128), F32),
            pltpu.SemaphoreType.DMA((4,)),
            pltpu.SemaphoreType.DMA((8,)),
            pltpu.SemaphoreType.DMA((2,)),
        ],
        compiler_params=pltpu.CompilerParams(vmem_limit_bytes=56 << 20),
        cost_estimate=pl.CostEstimate(flops=13_000_000_000, bytes_accessed=40_000_000, transcendentals=0),
        name="front",
    )(
        tokens, cot, tissue.reshape(images, 1, slots), vec["norm1_gain"], vec["norm1_shift"], qkv_w,
        vec["qkv_shift"], proj_w, vec["proj_shift"], vec["norm2_gain"], vec["norm2_shift"],
    )


OFFSETS = (0, 1, 4, 6, 7, 8, 9, 10, 12, 16)
TICKS = 4


class Exchange:
    def __init__(self, r):
        self.r = r
        self.dp = lax.axis_index("dp")
        self.core = lax.axis_index("fsdp")
        self.pending = []
        self.now = 0
        self.finals = []

    def side(self, bit):
        return (self.dp // bit) % 2

    def peer(self, bit):
        return (self.dp + bit * (1 - 2 * self.side(bit)), self.core)

    def other_core(self):
        return (self.dp, 1 - self.core)

    def greet(self):
        barrier = pltpu.get_barrier_semaphore()
        peers = [self.other_core()] + [self.peer(bit) for bit in (1, 2, 4, 8)]
        for peer in peers:
            pl.semaphore_signal(barrier, inc=1, device_id=peer, device_id_type=MESH)
        pl.semaphore_wait(barrier, len(peers))

    @staticmethod
    def bit_of(turn, k):
        if k == 3:
            return 8
        idx = (turn + k) % 3
        return 1 + idx + (idx * (idx - 1)) // 2

    def d_regions(self, u):
        start, size, out = 0, 256, []
        for k in range(4):
            bit = self.bit_of(u, k)
            side = self.side(bit)
            size //= 2
            out.append((bit, start + side * size, start + (1 - side) * size, size))
            start = start + side * size
        return out

    def d_copy(self, e, u):
        r = self.r
        sems = dict(send_sem=r.d_send.at[e, u], recv_sem=r.d_recv.at[e, u], device_id_type=MESH)
        if e == 0:
            src = r.d_stage.at[aligned((1 - self.core) * 256, 256, 256)]
            return pltpu.make_async_remote_copy(
                src_ref=src, dst_ref=r.d_core.at[u % 2], device_id=self.other_core(), **sems
            )
        k = e - 1 if e <= 4 else 8 - e
        bit, kept, sent, size = self.d_regions(u)[k]
        if e <= 4:
            src, dst = r.d_work.at[u % 2, aligned(sent, size, 16)], r.d_in[k].at[u]
        else:
            src = dst = r.d_total.at[aligned(u * 256 + kept, size, 16)]
        return pltpu.make_async_remote_copy(
            src_ref=src, dst_ref=dst, device_id=self.peer(bit), **sems
        )

    def d_event(self, e, u):
        r = self.r
        if e >= 1:
            self.d_copy(e - 1, u).wait()
        if e == 1:
            r.d_work[u % 2] = r.d_stage[aligned(self.core * 256, 256, 256)] + r.d_core[u % 2]
        elif 2 <= e <= 5:
            _, kept, _, size = self.d_regions(u)[e - 2]
            summed = r.d_work[u % 2, aligned(kept, size, 16)] + r.d_in[e - 2][u]
            if e < 5:
                r.d_work[u % 2, aligned(kept, size, 16)] = summed
            else:
                r.d_total[aligned(u * 256 + kept, size, 16)] = summed
        if e == 9:
            rows = aligned(u * 256, 256, 256)
            pltpu.make_async_copy(r.d_total.at[rows], r.d_out.at[rows], r.d_done.at[u]).start()
        else:
            self.d_copy(e, u).start()

    def u_blocks(self, u):
        width = self.r.width
        if not isinstance(u, int) or u < 6:
            return u * 256, 2 * width + u * 256
        tail = [4 * width + b * width + g * 256 for g in range(3) for b in range(3)]
        tail = [7 * width, 7 * width + 256, 7 * width + 512] + tail
        return tail[2 * (u - 6)], tail[2 * (u - 6) + 1]

    def u_regions(self, u):
        height = self.r.width // 2
        bits = [self.bit_of(u + 1, k) for k in range(4)]
        sides = [self.side(bit) for bit in bits]
        block, col, row = sides[0], sides[1] * 128, 0
        out = [
            (bits[0], (0, height, block, 0, 256), (0, height, 1 - block, 0, 256)),
            (bits[1], (0, height, block, col, 128), (0, height, block, 128 - col, 128)),
        ]
        for k in (2, 3):
            height //= 2
            kept, sent = row + sides[k] * height, row + (1 - sides[k]) * height
            out.append((bits[k], (kept, height, block, col, 128), (sent, height, block, col, 128)))
            row = kept
        return out

    @staticmethod
    def u_work(region):
        row, rows, block, col, cols = region
        return aligned(row, rows, 32), aligned(block * 256 + col, cols, 128)

    def u_place(self, u, region):
        row, rows, block, col, cols = region
        first, second = self.u_blocks(u)
        return aligned(row, rows, 32), aligned(first + block * (second - first) + col, cols, 128)

    def u_copy(self, e, u):
        r = self.r
        sems = dict(send_sem=r.u_send.at[e, u], recv_sem=r.u_recv.at[e, u], device_id_type=MESH)
        half = r.width // 2
        if e == 0:
            src = r.u_stage.at[u % 3, aligned((1 - self.core) * half, half, half)]
            return pltpu.make_async_remote_copy(
                src_ref=src, dst_ref=r.u_core.at[u % 3], device_id=self.other_core(), **sems
            )
        k = e - 1 if e <= 4 else 8 - e
        bit, kept, sent = self.u_regions(u)[k]
        if e <= 4:
            rows, cols = self.u_work(sent)
            src, dst = r.u_work.at[u % 4, rows, cols], r.u_in[k].at[u % 6]
        else:
            src = dst = r.u_total.at[self.u_place(u, kept)]
        return pltpu.make_async_remote_copy(
            src_ref=src, dst_ref=dst, device_id=self.peer(bit), **sems
        )

    def u_event(self, e, u):
        r = self.r
        half = r.width // 2
        if e >= 1:
            self.u_copy(e - 1, u).wait()
        if e == 1:
            r.u_work[u % 4] = r.u_stage[u % 3, aligned(self.core * half, half, half)] + r.u_core[u % 3]
        elif 2 <= e <= 5:
            _, kept, _ = self.u_regions(u)[e - 2]
            rows, cols = self.u_work(kept)
            summed = r.u_work[u % 4, rows, cols] + r.u_in[e - 2][u % 6]
            if e < 5:
                r.u_work[u % 4, rows, cols] = summed
            else:
                r.u_total[self.u_place(u, kept)] = summed
        if e == 9:
            for copy in self.u_outs(u):
                copy.start()
        else:
            self.u_copy(e, u).start()

    def u_outs(self, u):
        r = self.r
        return [
            pltpu.make_async_copy(
                r.u_total.at[:, aligned(col, 256, 256)],
                r.u_out.at[:, aligned(col, 256, 256)],
                r.u_done.at[n, u],
            )
            for n, col in enumerate(self.u_blocks(u))
        ]

    def v_copy(self, e):
        r = self.r
        peer = self.other_core() if e == 0 else self.peer(1 << (e - 1))
        return pltpu.make_async_remote_copy(
            src_ref=r.v_sum.at[e], dst_ref=r.v_in.at[e], send_sem=r.v_send.at[e],
            recv_sem=r.v_recv.at[e], device_id=peer, device_id_type=MESH,
        )

    def v_event(self, e, u=0):
        r = self.r
        if e >= 1:
            self.v_copy(e - 1).wait()
            r.v_sum[e] = r.v_sum[e - 1] + r.v_in[e - 1]
        if e < 5:
            self.v_copy(e).start()

    def loop_tick(self, c, j):
        for base, event in ((2, self.d_event), (3, self.u_event)):
            for e in range(9, 0, -1):
                back = base + OFFSETS[e] - j
                if back % TICKS == 0 and back // TICKS < 6:
                    d = back // TICKS

                    @pl.when(c >= d)
                    def _(event=event, e=e, d=d):
                        event(e, c - d)

    def after_loop(self, chunks):
        self.now = chunks * TICKS - 1
        for base, event in ((2, self.d_event), (3, self.u_event)):
            for u in range(chunks):
                for e in range(1, 10):
                    due = u * TICKS + base + OFFSETS[e]
                    if due > self.now:
                        self.pending.append((due, e, event, u))

    def begin_tail(self, u):
        self.u_event(0, u)
        for e in range(1, 10):
            self.pending.append((self.now + OFFSETS[e], e, self.u_event, u))

    def begin_vec(self):
        self.v_event(0)
        for e in range(1, 6):
            self.pending.append((self.now + e, e, self.v_event, 0))

    def tick(self):
        self.now += 1
        due = sorted((p for p in self.pending if p[0] <= self.now), key=lambda p: p[0])
        for p in due:
            self.run(p)

    def run(self, p):
        if p not in self.pending:
            return
        _, e, event, u = p
        if event == self.u_event and e == 1:
            for q in list(self.pending):
                if q[2] == self.u_event and (q[3] <= u - 6 or (q[3] <= u - 4 and q[1] <= 5)):
                    self.run(q)
        self.pending.remove(p)
        event(e, u)

    def drain(self):
        while self.pending:
            self.tick()
        for u in range(6):
            rows = aligned(u * 256, 256, 256)
            pltpu.make_async_copy(self.r.d_total.at[rows], self.r.d_out.at[rows], self.r.d_done.at[u]).wait()
        for u in range(12):
            for copy in self.u_outs(u):
                copy.wait()


class Local:
    def __init__(self, r):
        self.r = r
        self.copies = []

    def greet(self):
        pass

    def d_store(self, u):
        r = self.r
        outs = []
        for half in range(2):
            rows = aligned(half * 2 * r.width + u * 256, 256, 256)
            outs.append(
                pltpu.make_async_copy(r.d_stage.at[half * 256 : half * 256 + 256], r.d_out.at[rows], r.d_done.at[half])
            )
        return outs

    def d_event(self, e, u):
        for copy in self.d_store(u):
            copy.start()
        for copy in self.d_store(u):
            copy.wait()

    def u_event(self, e, u):
        r = self.r
        for n, col in enumerate(Exchange.u_blocks(self, u)):
            copy = pltpu.make_async_copy(
                r.u_stage.at[u % 3, :, n * 256 : n * 256 + 256],
                r.u_out.at[:, aligned(col, 256, 256)],
                r.u_done.at[n],
            )
            copy.start()
            copy.wait()

    def loop_tick(self, c, j):
        pass

    def after_loop(self, chunks):
        pass

    def begin_tail(self, u):
        self.u_event(0, u)

    def begin_vec(self):
        pass

    def tick(self):
        pass

    def drain(self):
        pass


class Refs:
    def __init__(self, names, refs):
        self.__dict__.update(zip(names, refs, strict=True))


def back_kernel(names, exchange, *refs):
    r = Refs(names, refs)
    rows_all, width = r.gs.shape
    r.width = width
    images = r.tb_hbm.shape[0]
    padded = rows_all // images
    chunks = r.up_b.shape[1] // 512
    if exchange:
        r.d_in = [r.d_in0, r.d_in1, r.d_in2, r.d_in3]
        r.u_in = [r.u_in0, r.u_in1, r.u_in2, r.u_in3]
    net = Exchange(r) if exchange else Local(r)

    def load(n, src, dst):
        copy = pltpu.make_async_copy(src, dst, r.load_sem.at[n])
        copy.start()
        return copy

    early = [load(0, r.s2_hbm, r.s), load(1, r.cot_hbm, r.cot), load(2, r.res_hbm, r.acc)]
    for b in range(4):
        src = r.up_hbm.at[:, b * width : (b + 1) * width]
        early.append(load(3 + b, src, r.w.at[b * width : (b + 1) * width]))
    early.append(load(7, r.down_hbm, r.w.at[4 * width : 8 * width]))
    late = [load(8, r.ho_hbm, r.h), load(10, r.tb_hbm, r.tb)]
    net.greet()
    r.gs[...] = jnp.zeros_like(r.gs)
    r.vec[...] = jnp.zeros_like(r.vec)
    for copy in early:
        copy.wait()

    def pt_copy(it, slot):
        g, half = it // 2, it % 2
        count = images // 2
        return pltpu.make_async_copy(
            r.pt_hbm.at[half * count : (half + 1) * count, g * 4 : g * 4 + 4],
            r.pt.at[slot],
            r.pt_sem.at[slot],
        )

    pt_copy(0, 0).start()

    @pl.loop(0, chunks)
    def _(c):
        half_cols = []
        block, col = c // 3, (c % 3) * 256
        for half in range(2):
            up_rows = aligned((2 * half + block) * width, width, width)
            down_rows = aligned(4 * width + half * 2 * width + c * 256, 256, 256)
            half_cols.append((up_rows, aligned(col, 256, 256), down_rows))
        for half in range(2):
            up_rows, up_cols, down_rows = half_cols[half]
            at = slice(half * 256, half * 256 + 256)
            bias = r.up_b[:, aligned(half * 2 * width + c * 256, 256, 256)]
            hidden = dot(r.s[...], r.w[up_rows, up_cols], 1, 0) + bias
            g_active = dot(r.cot[...], r.w[down_rows], 1, 1)
            active, slope = gelu_both(hidden)
            r.a[:, at] = active.astype(BF)
            g_hidden = (g_active * slope).astype(BF)
            r.b[:, at] = g_hidden
            sums = jnp.sum(g_hidden.astype(F32), axis=0, keepdims=True)
            r.vec[pl.ds(8 + 2 * half + block, 1), up_cols] = sums
        net.loop_tick(c, 0)
        for n in range(width // 256):
            at = slice(n * 256, n * 256 + 256)
            parts = []
            for half in range(2):
                up_rows, up_cols, down_rows = half_cols[half]
                left = slice(half * 256, half * 256 + 256)
                start = (2 * half + block) * width + n * 256
                parts.append(
                    (
                        dot(r.a[:, left], r.w[down_rows, at], 1, 0),
                        dot(r.b[:, left], r.w[aligned(start, 256, 256), up_cols], 1, 1),
                    )
                )
            r.acc[:, at] += parts[0][0] + parts[1][0]
            r.gs[:, at] += parts[0][1] + parts[1][1]
        net.loop_tick(c, 1)
        r.d_stage[...] = dot(r.a[:, :512], r.cot[...], 0, 0).astype(BF)
        net.d_event(0, c)
        net.loop_tick(c, 2)
        r.u_stage[c % 3] = dot(r.s[...], r.b[:, :512], 0, 0).astype(BF)
        net.u_event(0, c)
        net.loop_tick(c, 3)

    net.after_loop(chunks)
    late2 = []
    for b in range(3):
        src = r.qkv_hbm.at[:, b * width : (b + 1) * width]
        late2.append(load(3 + b, src, r.w.at[b * rows_all : (b + 1) * rows_all]))
    proj_rows = slice(3 * rows_all, 3 * rows_all + width)
    late2.append(load(6, r.proj_hbm, r.w.at[proj_rows]))
    late2.append(load(0, r.first_hbm, r.s))

    def res_copy(i, slot):
        return pltpu.make_async_copy(
            r.res_hbm.at[aligned(i * padded, padded, 16)], r.res.at[slot], r.res_sem.at[slot]
        )

    res_copy(0, 0).start()
    r.b[...] = (r.acc[...] + r.down_b[...]).astype(BF)
    out_copy = pltpu.make_async_copy(r.b, r.out_o, r.load_sem.at[7])
    out_copy.start()
    net.tick()

    def add_vec(n, value):
        r.vec[n : n + 1] += jnp.sum(value, axis=0, keepdims=True)

    @pl.loop(0, images)
    def _(i):
        slot = lax.rem(i, 2)
        res_copy(i, slot).wait()

        @pl.when(i + 1 < images)
        def _():
            res_copy(i + 1, 1 - slot).start()

        rows = aligned(i * padded, padded, 16)
        n, rstd = normalized(r.res[slot])
        grad = r.gs[rows]
        cot = r.cot[rows].astype(F32)
        add_vec(0, cot)
        add_vec(1, grad * n)
        add_vec(2, grad)
        t = grad * r.g2[...]
        centre = t - jnp.mean(t, axis=-1, keepdims=True) - n * jnp.mean(t * n, axis=-1, keepdims=True)
        g_res = cot + rstd * centre
        r.gs[rows] = g_res
        low = g_res.astype(BF)
        r.a[rows] = low
        add_vec(3, low.astype(F32))

    net.tick()
    for copy in late + late2:
        copy.wait()
    qkv_at = [r.cot.at[:width], r.cot.at[width : 2 * width], r.w.at[proj_rows]]
    qkv_src = [r.qkv_w_hbm.at[:, b * width : (b + 1) * width] for b in range(3)]
    qkv_loads = [load(3 + b, qkv_src[b], qkv_at[b]) for b in range(2)]
    for n in range(3):
        at = slice(n * 256, n * 256 + 256)
        p_grad = dot(r.h[...], r.a[:, at], 0, 0).astype(BF)
        r.u_stage[n // 2, :, n % 2 * 256 : n % 2 * 256 + 256] = p_grad
    net.begin_tail(6)
    net.tick()
    out_copy.wait()
    x_copy = load(8, r.x_hbm, r.h)
    for n in range(3):
        proj_at = slice(3 * rows_all + n * 256, 3 * rows_all + n * 256 + 256)
        g_heads = dot(r.a[...], r.w[proj_at], 1, 1)
        for i in range(images):
            rows = slice(i * padded, (i + 1) * padded)
            t = jnp.concatenate([r.tb[i]] * 2, axis=1)
            r.b[rows, n * 256 : n * 256 + 256] = (g_heads[rows] * t).astype(BF)
    qkv_loads.append(load(5, qkv_src[2], qkv_at[2]))
    net.tick()

    scaled = head_masks(0.125)
    ones = head_masks(1.0)
    stage = 1
    filled = 1
    for g in range(3):
        for half in range(2):
            it = 2 * g + half
            slot = it % 2
            pt_copy(it, slot).wait()
            if it < 5:
                pt_copy(it + 1, 1 - slot).start()
            for n in range(images // 2):
                i = half * (images // 2) + n
                for p in range(2):
                    cols = slice((2 * g + p) * 128, (2 * g + p + 1) * 128)
                    at = [slice(b * rows_all + i * padded, b * rows_all + (i + 1) * padded) for b in range(3)]
                    q, k, v = r.w[at[0], cols], r.w[at[1], cols], r.w[at[2], cols]
                    gh = r.b[i * padded : (i + 1) * padded, cols]
                    gq = gk = gv = None
                    for h in range(2):
                        low = r.pt[slot, n, 2 * p + h]
                        probs = low.astype(F32)
                        g_probs = dot(v * ones[h], gh, 1, 1)
                        row_dot = jnp.sum(probs * g_probs, axis=0, keepdims=True)
                        g_scores = (probs * (g_probs - row_dot)).astype(BF)
                        parts = (
                            dot(g_scores, k * scaled[h], 0, 0),
                            dot(g_scores, q * scaled[h], 1, 0),
                            dot(low, gh * ones[h], 1, 0),
                        )
                        gq, gk, gv = parts if gq is None else (gq + parts[0], gk + parts[1], gv + parts[2])
                    r.w[at[0], cols] = gq.astype(BF)
                    r.w[at[1], cols] = gk.astype(BF)
                    r.w[at[2], cols] = gv.astype(BF)
            net.tick()
        cols = slice(g * 256, (g + 1) * 256)
        for b in range(3):
            grads = r.w[b * rows_all : (b + 1) * rows_all, cols]
            r.u_stage[stage, :, filled * 256 : (filled + 1) * 256] = dot(r.s[...], grads, 0, 0).astype(BF)
            if b != 1:
                r.vec[4 + b // 2 : 5 + b // 2, cols] = jnp.sum(grads.astype(F32), axis=0, keepdims=True)
            filled += 1
            if filled == 2:
                net.begin_tail(6 + (3 * g + b + 3) // 2)
                stage, filled = (stage + 1) % 3, 0
        net.tick()

    x_copy.wait()
    for b in range(3):
        qkv_loads[b].wait()
        part = dot(r.w[b * rows_all : (b + 1) * rows_all], qkv_at[b][...], 1, 1)
        if b == 0:
            r.acc[...] = part
        else:
            r.acc[...] += part
        net.tick()

    @pl.loop(0, images)
    def _(i):
        rows = aligned(i * padded, padded, 16)
        n, rstd = normalized(r.h[rows].astype(F32))
        grad = r.acc[rows]
        add_vec(6, grad * n)
        add_vec(7, grad)
        t = grad * r.g1[...]
        centre = t - jnp.mean(t, axis=-1, keepdims=True) - n * jnp.mean(t * n, axis=-1, keepdims=True)
        r.a[rows] = (r.gs[rows] + rstd * centre).astype(BF)

    dx_copy = pltpu.make_async_copy(r.a, r.dx_o, r.load_sem.at[9])
    dx_copy.start()
    if exchange:
        r.v_sum[0] = r.vec[...]
    net.tick()
    net.begin_vec()
    net.drain()
    r.vec_o[...] = r.v_sum[5] if exchange else r.vec[...]
    dx_copy.wait()


def back(exchange, s2, res, cot, up, down, ho, proj_w, qkv, pt, first, qkv_w, x, tb, vec):
    rows, width = s2.shape
    images, padded = tb.shape[:2]
    hidden = up.shape[1]
    vm = pl.BlockSpec(memory_space=pltpu.VMEM)
    hbm = pl.BlockSpec(memory_space=pl.ANY)
    sds = jax.ShapeDtypeStruct
    half = width // 2
    if exchange:
        d_shape, u_shape = (hidden // 2, width), (half, 2 * hidden)
    else:
        d_shape, u_shape = (hidden, width), (width, 2 * hidden)
    ins = dict(
        s2_hbm=s2, res_hbm=res, cot_hbm=cot, up_hbm=up, down_hbm=down, ho_hbm=ho, proj_hbm=proj_w,
        qkv_hbm=qkv, pt_hbm=pt, first_hbm=first, qkv_w_hbm=qkv_w, x_hbm=x, tb_hbm=tb,
        up_b=vec["up_shift"], down_b=vec["down_shift"], g1=vec["norm1_gain"], g2=vec["norm2_gain"],
    )
    outs = dict(
        out_o=sds((rows, width), BF), dx_o=sds((rows, width), BF), d_out=sds(d_shape, BF),
        u_out=sds(u_shape, BF), vec_o=sds((16, width), F32),
    )
    dma = pltpu.SemaphoreType.DMA
    scratch = dict(
        s=pltpu.VMEM((rows, width), BF), cot=pltpu.VMEM((rows, width), BF), a=pltpu.VMEM((rows, width), BF),
        b=pltpu.VMEM((rows, width), BF), h=pltpu.VMEM((rows, width), BF), w=pltpu.VMEM((8 * width, width), BF),
        acc=pltpu.VMEM((rows, width), F32), gs=pltpu.VMEM((rows, width), F32),
        res=pltpu.VMEM((2, padded, width), F32),
        tb=pltpu.VMEM((images, padded, 128), F32), pt=pltpu.VMEM((2, images // 2, 4, padded, padded), BF),
        vec=pltpu.VMEM((16, width), F32), d_stage=pltpu.VMEM((512, width), BF),
        u_stage=pltpu.VMEM((3, width, 512), BF), load_sem=dma((11,)), res_sem=dma((2,)), pt_sem=dma((2,)),
    )
    if exchange:
        scratch.update(
            d_total=pltpu.VMEM(d_shape, BF), u_total=pltpu.VMEM(u_shape, BF),
            d_core=pltpu.VMEM((2, 256, width), BF), u_core=pltpu.VMEM((3, half, 512), BF),
            d_in0=pltpu.VMEM((6, 128, width), BF), d_in1=pltpu.VMEM((6, 64, width), BF),
            d_in2=pltpu.VMEM((6, 32, width), BF), d_in3=pltpu.VMEM((6, 16, width), BF),
            u_in0=pltpu.VMEM((6, half, 256), BF), u_in1=pltpu.VMEM((6, half, 128), BF),
            u_in2=pltpu.VMEM((6, half // 2, 128), BF), u_in3=pltpu.VMEM((6, half // 4, 128), BF),
            d_work=pltpu.VMEM((2, 256, width), BF), u_work=pltpu.VMEM((4, half, 512), BF),
            v_sum=pltpu.VMEM((6, 16, width), F32), v_in=pltpu.VMEM((5, 16, width), F32),
            d_send=dma((9, 6)), d_recv=dma((9, 6)), u_send=dma((9, 12)), u_recv=dma((9, 12)),
            v_send=dma((5,)), v_recv=dma((5,)), d_done=dma((6,)), u_done=dma((2, 12)),
        )
    else:
        scratch.update(d_done=dma((2,)), u_done=dma((2,)))
    small = {"up_b", "down_b", "g1", "g2"}
    params = dict(vmem_limit_bytes=63 << 20)
    if exchange:
        params.update(collective_id=1, has_side_effects=True)
    names = [*ins, *outs, *scratch]
    return pl.pallas_call(
        functools.partial(back_kernel, names, exchange),
        out_shape=list(outs.values()),
        in_specs=[vm if name in small else hbm for name in ins],
        out_specs=[hbm] * 4 + [vm],
        scratch_shapes=list(scratch.values()),
        compiler_params=pltpu.CompilerParams(**params),
        cost_estimate=pl.CostEstimate(flops=60_000_000_000, bytes_accessed=60_000_000, transcendentals=0),
        name="back",
    )(*ins.values())


def on_device(n_dp, n_fsdp, *args):
    names = (
        "tokens", "tissue", "norm1_gain", "norm1_shift", "qkv_matrix", "qkv_shift", "proj_matrix", "proj_shift",
        "norm2_gain", "norm2_shift", "up_matrix", "up_shift", "down_matrix", "down_shift", "cotangent",
    )
    arg = dict(zip(names, args, strict=True))
    images, slots, width = arg["tokens"].shape
    whole = {}
    for name in ("qkv_matrix", "proj_matrix", "up_matrix", "down_matrix"):
        whole[name] = lax.all_gather(arg[name], "fsdp", axis=0, tiled=True)
    vectors = [name for name in names if arg[name].ndim == 1]
    packed = lax.all_gather(jnp.concatenate([arg[name] for name in vectors]), "fsdp", axis=0)
    vec, at = {}, 0
    for name in vectors:
        size = arg[name].shape[0]
        vec[name] = packed[:, at : at + size].reshape(1, -1).astype(F32)
        at += size
    xp, cotp, first, qkv, pt, ho, res, s2, tb = front(
        arg["tokens"], arg["cotangent"], arg["tissue"], vec, whole["qkv_matrix"], whole["proj_matrix"]
    )
    exchange = n_dp == 16 and n_fsdp == 2
    out_p, dx_p, d_sum, u_sum, v_sum = back(
        exchange, s2, res, cotp, whole["up_matrix"], whole["down_matrix"], ho, whole["proj_matrix"], qkv, pt,
        first, whole["qkv_matrix"], xp, tb, vec,
    )
    hidden = arg["up_matrix"].shape[1]
    if not exchange:
        d_sum = lax.psum_scatter(d_sum, "fsdp", scatter_dimension=0, tiled=True)
        u_sum = lax.psum_scatter(u_sum, "fsdp", scatter_dimension=0, tiled=True)
        d_sum, u_sum = lax.psum((d_sum, u_sum), "dp")
        v_sum = lax.psum(v_sum, ("dp", "fsdp"))

    def own(v):
        size = v.shape[0] // n_fsdp
        return lax.dynamic_slice(v, (lax.axis_index("fsdp") * size,), (size,))

    def unpad(rows):
        return rows.reshape(images, -1, width)[:, :slots]

    return (
        unpad(out_p),
        unpad(dx_p),
        own(v_sum[6]),
        own(v_sum[7]),
        u_sum[:, hidden : hidden + 3 * width].astype(F32),
        own(v_sum[4:6].reshape(-1)),
        u_sum[:, hidden + 3 * width :].astype(F32),
        own(v_sum[3]),
        own(v_sum[1]),
        own(v_sum[2]),
        u_sum[:, :hidden].astype(F32),
        own(v_sum[8:12].reshape(-1)),
        d_sum.astype(F32),
        own(v_sum[0]),
    )


def solution(mesh):
    rows = P(("dp", "fsdp"), None, None)
    vec, mat = P("fsdp"), P("fsdp", None)
    weights = (vec, vec, mat, vec, mat, vec, vec, vec, mat, vec, mat, vec)
    return jax.shard_map(
        functools.partial(on_device, mesh.shape["dp"], mesh.shape["fsdp"]),
        mesh=mesh,
        in_specs=(rows, P(("dp", "fsdp"), None)) + weights + (rows,),
        out_specs=(rows, rows) + weights,
        check_vma=False,
    )
```

time: 677 us -> 320 us (0.47)
  matrix products: 255 us -> 0 us
  Pallas kernels: 0 us -> 254 us
  other arithmetic: 135 us -> 10.3 us
  waiting for transfers between devices: 127 us -> 16.8 us
  blocking collectives: 98.9 us -> 2.37 us
  local copies, waits for them, and re-layouts: 37.7 us -> 19.2 us
    dot_general x36 -> x0, matrix products: 255 us -> none  [the longest x8 70.9 us: product_back(): jnp.einsum('bpe,de->bpd', rows_in, matrix, preferred_element_type=jnp.flo...]
    pallas_call x0 -> x2, Pallas kernels: none -> 254 us  [the longest x1 221 us: back(): pl.pallas_call(functools.partial(back_kernel, names, exchange), out_shape...]
    psum x1 -> x0, waiting for transfers between devices: 110 us -> none  [on_device(): lax.psum(owned[2].astype(jnp.bfloat16), 'dp').astype(jnp.float32)]
    convert_element_type x37 -> x4, other arithmetic: 112 us -> 10.3 us  [the longest x1 4.57 us: on_device(): u_sum[:, :hidden].astype(F32)]
    psum x1 -> x0, blocking collectives: 80.4 us -> none  [on_device(): lax.psum(owned[0].astype(jnp.bfloat16), 'dp').astype(jnp.float32)]
    reduce_sum x14 -> x0, other arithmetic: 22.3 us -> none  [the longest x5 10.6 us: column_sum(): return jnp.sum(matrix_rows.astype(jnp.float32), axis=(0, 1))]
    convert_element_type x10 -> x0, local copies, waits for them, and re-layouts: 14.5 us -> none  [the longest x2 13.1 us: run_forward(): qkv_rows = (product(first_in, qkv_matrix) + shift_all).astype(jnp.bfloat16)]
    all_gather x4, waiting for transfers between devices: 0.05 us -> 14.2 us  [on_device(): whole[name] = lax.all_gather(arg[name], 'fsdp', axis=0, tiled=True)]
  transfers between devices with their start and end apart: 13 -> 4, of which waited for: 2 -> 2; matrix products, arithmetic and copies ran while one was open for 52% -> 3% of each run, Pallas kernels for 0% -> 11%
where the time goes in v1:
time: 320 us; the launch traced here: 317 us
  Pallas kernels  254 us (79%)
  local copies, waits for them, and re-layouts  19.2 us (6%)
  waiting for transfers between devices  16.8 us (5%)
  between operations  14.2 us (4%)
  other arithmetic  10.3 us (3%)
    pallas_call x1, Pallas kernels, back(): pl.pallas_call(functools.partial(back_kernel, names, exchange), out_shape...  221 us
    pallas_call x1, Pallas kernels, front(): pl.pallas_call(front_kernel, out_shape=[sds((rows, width), BF), sds((rows...  33.6 us
    unnamed x53, local copies, waits for them, and re-layouts  14.9 us
    all_gather x4, waiting for transfers between devices, on_device(): whole[name] = lax.all_gather(arg[name], 'fsdp', axis=0, tiled=True)  14.2 us
  transfers between devices with their start and end apart: 4, of which 2 were waited for; matrix products, arithmetic and copies ran while one was open for 3% of the time, Pallas kernels for 11%

profile of v1, /device:TPU:0, one launch (start us, length us, event | category | flops | bytes accessed | tf_op | source)
XLA Modules:
  0.0 317.1 jit_solution(1594581988603375695)
XLA Ops:
  7.2 0.7 all-gather.9.cloned.1.call-update
  8.0 0.7 all-gather.7.cloned.1.call-update
  8.8 0.7 all-gather.11.cloned.1.call-update
  11.9 2.4 all-gather.1
  17.3 0.6 copy.46
  17.9 1.9 copy.37.x_hbm
  19.8 1.9 copy.38.cot_hbm
  21.7 0.6 reshape.169.tissue
  22.9 0.6 copy.50
  23.5 13.5 %all-gather.7.cloned.1.call-done.qkv_w_hbm.refs_10_ = bf16[768,2304]{1,0:T(8,128)(2,1)} async-done(((bf16[384,2304]{1,0:T(8,128)(2,1)}), bf16[768,2304]{1,0:T(8,128)(2,1)}) %all-gather.7.cloned.1.call-update) | async-done | bytes 3538960 | tf_op jit(solution)/shard_map/all_gather | solution.py:818
  37.0 33.6 %front.1 = (bf16[1664,768]{1,0:T(8,128)(2,1)}, bf16[1664,768]{1,0:T(8,128)(2,1)}, bf16[1664,768]{1,0:T(8,128)(2,1)}, bf16[1664,2304]{1,0:T(8,128)(2,1)}, bf16[8,...) custom-call(bf16[8,196,768]{2,1,0:T(8,128)(2,1)} %copy.37.x_hbm, ...), custom_call_target="tpu_custom_call" | custom-call | flops 12999999488 | bytes 40000000 | tf_op jit(solution)/shard_map/front/pallas_call | solution.py:168
  70.6 0.6 all-gather.13.cloned.1.call-done.refs_4_
  71.3 220.5 %back.1 = (bf16[1664,768]{1,0:T(8,128)(2,1)}, bf16[1664,768]{1,0:T(8,128)(2,1)}, bf16[1536,768]{1,0:T(8,128)(2,1)}, bf16[384,6144]{1,0:T(8,128)(2,1)}, f32[16,768]{1,0:T(8,128)}) custom-call(bf16[1664,768]{1,0:T(8,128)(2,1)} %get-tuple-element.28.refs_0_, f32[1664,768]{1,0:T(8,128)} %get-tuple-element.29.refs_1_, ...), custom_call_target="tpu_custom_call" | custom-call | flops 60000002048 | bytes 60000000 | tf_op jit(solution)/shard_map/back/pallas_call | solution.py:797
  291.8 4.6 %slice_convert_fusion = f32[384,3072]{1,0:T(8,128)} fusion(bf16[384,6144]{1,0:T(8,128)(2,1)} %get-tuple-element.40), kind=kLoop, calls=%fused_computation | loop fusion | flops 1179648 | bytes 7077888 | tf_op jit(solution)/shard_map/convert_element_type | solution.py:859
  296.4 2.1 slice_convert_fusion.1
  298.5 1.1 slice_convert_fusion.2
  299.8 1.9 copy.42
  302.4 1.9 copy.43
  304.6 2.5 convert_element_type.71
  307.2 0.6 dynamic-slice_reduce_fusion
  307.8 0.6 dynamic-slice_reduce_fusion.2
  308.4 0.6 dynamic-slice_reduce_fusion.4
  309.0 0.7 dynamic_slice.47
  309.7 0.7 dynamic_slice.40
  (66 shorter events, 7.4 us)
Async XLA Ops:
  7.2 16.3 %all-gather.9.cloned.1.call-start = ((), (), s32[]{:S(2)}) async-start(), calls=%async_computation.1 | async-start | bytes 1769472 | tf_op jit(solution)/shard_map/all_gather | solution.py:818
  7.9 29.1 %all-gather.7.cloned.1.call-start = ((), (), s32[]{:S(2)}) async-start(), calls=%async_computation | async-start | bytes 5308416 | tf_op jit(solution)/shard_map/all_gather | solution.py:818
  8.7 1.4 copy-start.10
  8.7 1.7 copy-start.11
  8.7 1.9 copy-start.9
  8.7 2.1 copy-start.12
  8.7 2.3 copy-start.13
  8.7 2.5 copy-start.14
  8.7 2.7 copy-start.8
  8.7 3.0 copy-start.15
  8.7 9.1 %copy-start.1 = (bf16[8,196,768]{2,0,1:T(8,128)(2,1)S(1)}, bf16[8,196,768]{2,0,1:T(8,128)(2,1)}, u32[]{:S(2)}) copy-start(bf16[8,196,768]{2,0,1:T(8,128)(2,1)} %param.15) | copy-start | bytes 7225348
  8.8 61.9 %all-gather.11.cloned.1.call-start = ((), (), s32[]{:S(2)}) async-start(), calls=%async_computation.2 | async-start | bytes 7077888 | tf_op jit(solution)/shard_map/all_gather | solution.py:818
  9.5 61.8 %all-gather.13.cloned.1.call-start = ((), (), s32[]{:S(2)}) async-start(), calls=%async_computation.3 | async-start | bytes 7077888 | tf_op jit(solution)/shard_map/all_gather | solution.py:818
  11.9 7.8 %copy-start.2 = (bf16[8,196,768]{2,0,1:T(8,128)(2,1)S(1)}, bf16[8,196,768]{2,0,1:T(8,128)(2,1)}, u32[]{:S(2)}) copy-start(bf16[8,196,768]{2,0,1:T(8,128)(2,1)} %param.29) | copy-start | bytes 7225348
  19.8 1.9 copy-start.7
  291.8 4.6 %copy-start = (bf16[384,6144]{1,0:T(8,128)(2,1)S(1)}, bf16[384,6144]{1,0:T(8,128)(2,1)}, u32[]{:S(2)}) copy-start(bf16[384,6144]{1,0:T(8,128)(2,1)} %get-tuple-element.40) | copy-start | bytes 14155780
  296.4 3.2 %copy-start.6 = (f32[16,768]{1,0:T(8,128)S(1)}, f32[16,768]{1,0:T(8,128)}, u32[]{:S(2)}) copy-start(f32[16,768]{1,0:T(8,128)} %get-tuple-element.39) | copy-start | bytes 147460
  296.4 3.2 %copy-start.4 = (bf16[1664,768]{1,0:T(8,128)(2,1)S(1)}, bf16[1664,768]{1,0:T(8,128)(2,1)}, u32[]{:S(2)}) copy-start(bf16[1664,768]{1,0:T(8,128)(2,1)} %get-tuple-element.37) | copy-start | bytes 7667716
  299.8 2.4 copy-start.3
  302.4 2.2 copy-start.5
Sparse Core Ops, SparseCore 0:
  9.6 11.9 all-gather.8
  23.1 13.8 all-gather.6
  38.6 15.6 all-gather.10
  55.6 15.6 all-gather.12
